TPU v7x, 32 devices: a whole 2x2x4 slice. The times are simulated.
32 devices in a mesh: grp: 4 (over y, x), tok: 8 (over z, core).
Axes of the slice: x: 2, y: 2, z: 4, core: 2. Of those that a mesh axis runs over, the one named last changes fastest.
Arguments:
- hidden_in: bfloat16 [4, 2048, 2048], P('grp', 'tok'), may hold values from -6 to 6
- doc_ids: int32 [4, 2048], P('grp', 'tok'), may hold values from 0 to 7, never falling along the last dimension, each value on 1 to 512 neighbouring positions
- prefix_kv: bfloat16 [4, 256, 1024], P('grp', 'tok'), may hold values from -1024 to 1024
- prefix_owner: int32 [4], replicated, may hold values from 0 to 3, each once
- norm_gain: bfloat16 [2048], replicated, may hold values from 0.5 to 2
- query_gain: bfloat16 [128], replicated, may hold values from 0.59765625 to 2.390625
- key_norm_gain: bfloat16 [128], replicated, may hold values from 0.59765625 to 2.390625
- w_qkv: bfloat16 [2048, 2048], P('tok'), may hold values from -0.125 to 0.125
- w_out: bfloat16 [1024, 2048], P('tok'), may hold values from -0.1875 to 0.1875
Outputs:
- attn_out: bfloat16 [4, 2048, 2048], P('grp', 'tok')
- key_cache: bfloat16 [4, 2048, 512], P('grp', 'tok')
- value_cache: bfloat16 [4, 2048, 512], P('grp', 'tok')
Inputs may be any that keep to these rules, and one draw needn't show every extreme that they name: `doc_ids`: in each group the ids never fall; every one of the 8 requests has 1 to 512 tokens, and one has exactly 512. `prefix_owner`: A permutation of the groups.
All inputs are finite; a program needn't handle non-finite values.
Results may differ from a plain program's by a relative error of at most 0.013.
The roundings to bfloat16 on the way count: a program that leaves them out, or rounds other values in their place, can miss the bound.
Values may be sent and summed in bfloat16 or wider, within the bound.
A program may use at most 128 MiB of HBM per device.

v0:
```python
import jax
import jax.numpy as jnp
from jax import lax
from jax.sharding import PartitionSpec as P

SPAN_DEV = 2


epsilon = 1e-06
theta_base = 1000000.0
floor_score = -1e30


def entering(x, axis, combine, identity):
    length, index = (lax.axis_size(axis), lax.axis_index(axis))
    everything = jax.tree.map(lambda part: lax.all_gather(part, axis), x)
    start = jax.tree.map(
        lambda part, zero: jnp.broadcast_to(jnp.asarray(zero, part.dtype), part.shape), x, identity
    )

    def hop(k, before):
        reached = k < index
        new = combine(before, jax.tree.map(lambda part: part[k], everything))
        return jax.tree.map(lambda a, b: jnp.where(reached, a, b), new, before)

    return lax.fori_loop(0, length, hop, start)


def shifted(block, axis, distance):
    devices = range(lax.axis_size(axis))
    route = [(i - distance, i) for i in devices if i - distance in devices]
    return lax.ppermute(block, axis, route)


def root_mean_scale(value_heads):
    return value_heads * lax.rsqrt(
        jnp.mean(value_heads * value_heads, axis=-1, keepdims=True) + epsilon
    )


def rotary_embed(heads, token_positions):
    half_width = heads.shape[-1] // 2
    freqs = theta_base ** (-jnp.arange(half_width, dtype=jnp.float32) / half_width)
    angles = token_positions[:, None] * freqs[None, :]
    cosine = jnp.cos(angles)[:, None, :]
    sine = jnp.sin(angles)[:, None, :]
    first = heads[..., :half_width]
    second = heads[..., half_width:]
    return jnp.concatenate(
        [first * cosine - second * sine, second * cosine + first * sine], axis=-1
    )


def attend(query_heads, key_heads, value_heads, allowed, scale):
    scores = (
        jnp.einsum("rgjd,kgd->gjrk", query_heads, key_heads, preferred_element_type=jnp.float32)
        * scale
    )
    scores = jnp.where(allowed[None, None], scores, floor_score)
    top = jnp.max(scores, axis=-1)
    weights = jnp.where(allowed[None, None], jnp.exp(scores - top[..., None]), 0.0)
    total = jnp.sum(weights, axis=-1)
    mixed = jnp.einsum(
        "gjrk,kgd->gjrd",
        weights.astype(jnp.bfloat16),
        value_heads,
        preferred_element_type=jnp.float32,
    )
    return (top, total, mixed)


def combine_parts(first, second):
    top = jnp.maximum(first[0], second[0])
    left = jnp.exp(first[0] - top)
    right = jnp.exp(second[0] - top)
    return (
        top,
        first[1] * left + second[1] * right,
        first[2] * left[..., None] + second[2] * right[..., None],
    )


def join_runs(earlier, later):
    link = earlier[1] == later[0]
    tail_joined = jnp.where((later[3] == 1) & link, earlier[2] + later[2], later[2])
    uniform_joined = earlier[3] * later[3] * link.astype(jnp.int32)
    joined = (earlier[0], later[1], tail_joined, uniform_joined)
    earlier_empty = earlier[1] < 0
    later_empty = later[1] < 0
    return tuple(
        (
            jnp.where(earlier_empty, b_item, jnp.where(later_empty, a_item, c_item))
            for a_item, b_item, c_item in zip(earlier, later, joined)
        )
    )


def per_device(
    hidden_in, doc_ids, prefix_kv, prefix_owner, norm_gain, query_gain, key_norm_gain, w_qkv, w_out
):
    rows = hidden_in.shape[1]
    head_dim = query_gain.shape[0]
    key_value_width = prefix_kv.shape[2] // 2
    kv_heads = key_value_width // head_dim
    qkv_width = w_qkv.shape[1]
    query_width = qkv_width - 2 * key_value_width
    q_heads = query_width // head_dim
    group_ratio = q_heads // kv_heads
    pre_rows = prefix_kv.shape[1]
    prefix_len = pre_rows * lax.axis_size("tok")
    scale = head_dim ** (-0.5)
    tokens = hidden_in[0].astype(jnp.float32)
    normed = (root_mean_scale(tokens) * norm_gain.astype(jnp.float32)).astype(jnp.bfloat16)
    columns = normed
    query_key_value = jnp.dot(
        columns,
        lax.all_gather(w_qkv, "tok", axis=0, tiled=True),
        preferred_element_type=jnp.float32,
    )
    ids = doc_ids[0]
    first_id = ids[0]
    last_id = ids[-1]
    tail_count = jnp.sum((ids == last_id).astype(jnp.int32))
    uniform = (first_id == last_id).astype(jnp.int32)
    blank = jnp.array(-1, jnp.int32)
    identity = (blank, blank, jnp.array(0, jnp.int32), jnp.array(1, jnp.int32))
    before = entering((first_id, last_id, tail_count, uniform), "tok", join_runs, identity)
    index = jnp.arange(rows, dtype=jnp.int32)
    changed = jnp.concatenate([jnp.ones((1,), dtype=jnp.bool_), ids[1:] != ids[:-1]])
    run_start = lax.cummax(jnp.where(changed, index, 0), axis=0)
    offset = index - run_start + jnp.where(ids == before[1], before[2], 0)
    token_positions = (prefix_len + offset).astype(jnp.float32)
    query_heads = rotary_embed(
        root_mean_scale(query_key_value[:, :query_width].reshape(rows, q_heads, head_dim))
        * query_gain.astype(jnp.float32),
        token_positions,
    ).astype(jnp.bfloat16)
    key_heads = rotary_embed(
        root_mean_scale(
            query_key_value[:, query_width : query_width + key_value_width].reshape(
                rows, kv_heads, head_dim
            )
        )
        * key_norm_gain.astype(jnp.float32),
        token_positions,
    ).astype(jnp.bfloat16)
    value_flat = query_key_value[:, query_width + key_value_width :].astype(jnp.bfloat16)
    key_flat = key_heads.reshape(rows, key_value_width)
    value_heads = value_flat.reshape(rows, kv_heads, head_dim)
    grouped_queries = query_heads.reshape(rows, kv_heads, group_ratio, head_dim)
    owners = lax.all_gather(prefix_kv[0], "grp", axis=0, tiled=True)
    own_rows = lax.dynamic_slice_in_dim(
        owners, prefix_owner[lax.axis_index("grp")] * pre_rows, pre_rows, 0
    )
    empty_part = (
        jnp.full((kv_heads, group_ratio, rows), floor_score, jnp.float32),
        jnp.zeros((kv_heads, group_ratio, rows), jnp.float32),
        jnp.zeros((kv_heads, group_ratio, rows, head_dim), jnp.float32),
    )
    piece = lax.all_gather(own_rows, "tok", axis=0, tiled=True)
    piece_keys = piece[:, :key_value_width].reshape(piece.shape[0], kv_heads, head_dim)
    piece_values = piece[:, key_value_width:].reshape(piece.shape[0], kv_heads, head_dim)
    add_allowed = jnp.ones((rows, piece.shape[0]), dtype=jnp.bool_)
    state = combine_parts(
        empty_part, attend(grouped_queries, piece_keys, piece_values, add_allowed, scale)
    )
    own_allowed = (ids[:, None] == ids[None, :]) & (index[None, :] <= index[:, None])
    state = combine_parts(
        state, attend(grouped_queries, key_heads, value_heads, own_allowed, scale)
    )
    marks = ids + 1
    joined_kv = jnp.concatenate([key_flat, value_flat], axis=1)
    for back in range(1, SPAN_DEV + 1):
        got_kv, got_marks = shifted((joined_kv, marks), "tok", back)
        got_keys = got_kv[:, :key_value_width].reshape(rows, kv_heads, head_dim)
        got_values = got_kv[:, key_value_width:].reshape(rows, kv_heads, head_dim)
        allowed = marks[:, None] == got_marks[None, :]
        state = combine_parts(state, attend(grouped_queries, got_keys, got_values, allowed, scale))
    mixed = state[2] / state[1][..., None]
    attended = jnp.transpose(mixed, (2, 0, 1, 3)).reshape(rows, query_width).astype(jnp.bfloat16)
    columns = attended
    projected = jnp.dot(
        columns,
        lax.all_gather(w_out, "tok", axis=0, tiled=True),
        preferred_element_type=jnp.float32,
    )
    return (projected.astype(jnp.bfloat16)[None], key_flat[None], value_flat[None])


def solution(mesh):
    return jax.shard_map(
        per_device,
        mesh=mesh,
        in_specs=(
            P("grp", "tok", None),
            P("grp", "tok"),
            P("grp", "tok", None),
            P(),
            P(),
            P(),
            P(),
            P("tok", None),
            P("tok", None),
        ),
        out_specs=(P("grp", "tok", None), P("grp", "tok", None), P("grp", "tok", None)),
        check_vma=False,
    )
```

profile of v0, /device:TPU:1, one launch (start us, length us, event | category | flops | bytes accessed | tf_op | source)
XLA Modules:
  0.0 180.2 jit_solution(8446390135132782549)
XLA Ops:
  7.2 0.7 all-gather.7.cloned.1.call-update
  8.0 1.3 fusion.98
  10.5 1.2 dynamic-slice.1
  11.8 1.3 bitcast_dynamic-update-slice_fusion.1
  13.1 1.3 bitcast_dynamic-update-slice_fusion
  14.5 2.0 %fusion.76 = s32[]{:T(128)} fusion(s32[256]{0:T(256)} %bitcast.271, s32[]{:T(128)} %bitcast.15), kind=kLoop, calls=%fused_computation.126 | loop fusion | flops 767 | bytes 1032 | tf_op jit(solution)/shard_map/reduce_sum | solution.py:123
  16.4 1.4 dynamic-update-slice.1
  17.8 0.8 dynamic-update-slice.2
  18.6 9.4 %all-reduce.4 = (s32[8]{0:T(128)S(1)}, s32[8]{0:T(128)S(1)}, s32[8]{0:T(128)S(1)}, s32[8]{0:T(128)S(1)}) all-reduce(s32[8]{0:T(128)S(1)} %bitcast_dynamic-update-slice_fusion.1, s32[8]{0:T(128)S(1)} %dynamic-update-slice.1, s32[8]{0:T(128)S(1)} %dynamic-update-slice.2, ...), channel_id=3, replica_groups=mesh['grp'=4,'tok'=8] {'tok'}, use_global_device_ids=true, to_apply=%add | all-reduce | flops 32 | bytes 256 | tf_op jit(solution)/shard_map/all_gather | solution.py:16
  27.9 0.8 compare_reduce_fusion
  29.3 60.0 %while.15 = (s32[]{:T(128)}, s32[]{:T(128)}, s32[]{:T(128)}, s32[]{:T(128)}, s32[8]{0:T(128)S(1)}, /*index=5*/s32[8]{0:T(128)S(1)}, s32[8]{0:T(128)S(1)}, s32[8]...) while((s32[]{:T(128)}, s32[]{:T(128)}, s32[]{:T(128)}, s32[]{:T(128)}, s32[8]{0:T(128)S(1)}, ...), condition=%wide.region_6.7_spmd, body=%wide.region_5.6_spmd.sunk | while | flops 16 | bytes 324 | solution.py:26
  31.8 0.6 dynamic_slice.41
  32.4 0.6 dynamic_slice.42
  33.7 0.6 dynamic_slice.43
  39.3 0.6 dynamic_slice.41
  39.9 0.6 dynamic_slice.42
  41.2 0.6 dynamic_slice.43
  46.8 0.6 dynamic_slice.41
  47.4 0.6 dynamic_slice.42
  48.7 0.6 dynamic_slice.43
  54.4 0.6 dynamic_slice.41
  55.0 0.6 dynamic_slice.42
  56.2 0.6 dynamic_slice.43
  61.9 0.6 dynamic_slice.41
  62.5 0.6 dynamic_slice.42
  63.7 0.6 dynamic_slice.43
  69.4 0.6 dynamic_slice.41
  71.2 0.6 dynamic_slice.43
  76.9 0.6 dynamic_slice.41
  78.7 0.6 dynamic_slice.43
  84.4 0.6 dynamic_slice.41
  85.0 0.6 dynamic_slice.42
  86.2 0.6 dynamic_slice.43
  89.4 0.8 broadcast_add_fusion
  90.2 3.9 %collective-permute-start = (s32[256]{0:T(256)S(1)}, s32[256]{0:T(256)S(1)}, u32[]{:S(2)}, u32[]{:S(2)}) collective-permute-start(s32[256]{0:T(256)S(1)} %get-tuple-element.203), channel_id=1, source_target_pairs={{0,1},{1,2},{2,3},{3,4},{4,5},{5,6},{6,7},{8,9},{9,10},{10,11},{11... | collective-permute-start | bytes 3080 | tf_op jit(solution)/shard_map/ppermute | solution.py:32
  94.1 2.0 %collective-permute-start.2 = (s32[256]{0:T(256)S(1)}, s32[256]{0:T(256)S(1)}, u32[]{:S(2)}, u32[]{:S(2)}) collective-permute-start(s32[256]{0:T(256)S(1)} %get-tuple-element.203), channel_id=1, source_target_pairs={{0,2},{1,3},{2,4},{3,5},{4,6},{5,7},{8,10},{9,11},{10,12},{11,13},... | collective-permute-start | bytes 3080 | tf_op jit(solution)/shard_map/ppermute | solution.py:32
  96.1 1.5 fusion.62
  97.9 7.0 %all-gather = bf16[1,128,1024]{2,1,0:T(8,128)(2,1)S(1)} all-gather(bf16[1,32,1024]{2,1,0:T(8,128)(2,1)S(1)} %copy-done.10), channel_id=2, replica_groups=mesh['grp'=4,'tok'=8] {'grp'}, dimensions={1}, use_global_device_ids=true | all-gather | bytes 327680 | tf_op jit(solution)/shard_map/all_gather | solution.py:151
  106.1 19.0 %all-gather.3 = bf16[1,256,1024]{2,1,0:T(8,128)(2,1)S(1)} all-gather(bf16[1,32,1024]{2,1,0:T(8,128)(2,1)S(1)} %constant_dynamic-slice_fusion), channel_id=5, replica_groups=mesh['grp'=4,'tok'=8] {'tok'}, dimensions={1}, use_global_device_ids=true | all-gather | bytes 589824 | tf_op jit(solution)/shard_map/all_gather | solution.py:160
  125.4 0.7 fusion.96
  126.9 5.8 %fusion.33 = f32[256,2048]{1,0:T(8,128)S(1)} fusion(bf16[2048,2048]{1,0:T(8,128)(2,1)} %all-gather.7.cloned.1.call-done, bf16[1,256,2048]{2,1,0:T(8,128)(2,1)S(1)} %copy-done.3, f32[2048]{0:T(1024)S(1)} %convert_element_type.72, f32[256]{0:T(256)S(1)} %add_rsqrt_fusion.2), kind=kOutput, calls=%fused_computation.44 | convolution fusion | flops 2149580800 | bytes 11543552 | tf_op jit(solution)/shard_map/dot_general | solution.py:115
  132.9 1.2 copy-done.1
  135.4 0.9 pad_maximum_fusion.1
  136.3 2.1 %collective-permute-start.3 = (bf16[256,1024]{1,0:T(8,128)(2,1)}, bf16[256,1024]{1,0:T(8,128)(2,1)}, u32[]{:S(2)}, u32[]{:S(2)}) collective-permute-start(bf16[256,1024]{1,0:T(8,128)(2,1)} %pad_maximum_fusion.1), channel_id=1, source_target_pairs={{0,2},{1,3},{2,4},{3,5},{4,6},{5,7},{8,10},{9,11},{10,12},{11,13},... | collective-permute-start | bytes 1572872 | tf_op jit(solution)/shard_map/ppermute | solution.py:32
  138.4 3.0 %collective-permute-start.1 = (bf16[256,1024]{1,0:T(8,128)(2,1)}, bf16[256,1024]{1,0:T(8,128)(2,1)}, u32[]{:S(2)}, u32[]{:S(2)}) collective-permute-start(bf16[256,1024]{1,0:T(8,128)(2,1)} %pad_maximum_fusion.1), channel_id=1, source_target_pairs={{0,1},{1,2},{2,3},{3,4},{4,5},{5,6},{6,7},{8,9},{9,10},{10,11},{11... | collective-permute-start | bytes 1572872 | tf_op jit(solution)/shard_map/ppermute | solution.py:32
  143.8 1.8 %slice_bitcast_fusion.2 = bf16[1,256,512]{2,1,0:T(8,128)(2,1)} fusion(f32[256,2048]{1,0:T(8,128)} %copy-done.1), kind=kLoop, calls=%fused_computation.154 | loop fusion | bytes 524288 | tf_op jit(solution)/shard_map/broadcast_in_dim | solution.py:187
  146.1 1.8 %fusion.5 = (f32[4,2,256]{2,1,0:T(2,128)S(1)}, f32[4,256,256,2]{2,1,3,0:T(8,128)}) fusion(pred[256,256]{0,1:T(8,128)(4,1)S(1)} %copy-done.5, bf16[256,4,2,128]{3,0,2,1:T(8,128)(2,1)S(1)} %pad_maximum_fusion, bf16[256,4,128]{2,0,1:T(8,128)(2,1)S(1)} %maximum_convert_fusion), kind=kOutput, calls=%fused_computation.16 | convolution fusion | flops 135788544 | bytes 2957312 | tf_op jit(solution)/shard_map/rgjd,kgd->gjrk/dot_general | solution.py:56
  147.9 0.6 exponential_multiply_fusion
  148.5 1.0 fusion.8
  149.5 0.9 copy.114
  150.5 0.8 copy.99
  151.4 2.7 %fusion.10 = f32[4,2,256]{2,1,0:T(2,128)} fusion(f32[4,256,256,2]{2,1,3,0:T(8,128)} %get-tuple-element.212, f32[4,2,256]{2,1,0:T(2,128)S(1)} %get-tuple-element.211, pred[256,256]{0,1:T(8,128)(4,1)} %fusion.62), kind=kLoop, calls=%fused_computation.21 | loop fusion | flops 2619392 | bytes 2179072 | tf_op jit(solution)/shard_map/reduce_sum | solution.py:62
  154.1 1.1 fusion.97
  155.1 0.8 copy.120
  156.0 1.8 %collective-permute-done.1 = bf16[256,1024]{1,0:T(8,128)(2,1)} collective-permute-done((bf16[256,1024]{1,0:T(8,128)(2,1)}, bf16[256,1024]{1,0:T(8,128)(2,1)}, u32[]{:S(2)}, u32[]{:S(2)}) %collective-permute-start.1) | collective-permute-done | bytes 524320 | tf_op jit(solution)/shard_map/ppermute | solution.py:32
  157.9 1.9 %fusion.95 = (bf16[256,512]{1,0:T(8,128)(2,1)}, bf16[256,512]{1,0:T(8,128)(2,1)}) fusion(bf16[256,1024]{1,0:T(8,128)(2,1)} %collective-permute-done.1), kind=kLoop, calls=%fused_computation.150 | loop fusion | bytes 1048576 | tf_op jit(solution)/shard_map/slice | solution.py:176
  159.8 1.0 reshape.386
  160.8 1.8 %copy.117 = bf16[256,512]{0,1:T(8,128)(2,1)} copy(bf16[256,512]{1,0:T(8,128)(2,1)} %get-tuple-element.190) | data formatting | bytes 524288 | tf_op jit(solution)/shard_map/reshape | solution.py:176
  163.7 1.1 fusion.12
  164.8 0.7 fusion.27
  165.5 0.9 copy-done
  166.4 0.7 fusion.21
  168.1 0.8 fusion.28
  168.9 4.4 %fusion = bf16[1,256,2048]{2,1,0:T(8,128)(2,1)} fusion(bf16[256,1024]{0,1:T(8,128)(2,1)S(1)} %bitcast.274, bf16[1024,2048]{1,0:T(8,128)(2,1)} %all-gather.9.cloned.1.call-done), kind=kOutput, calls=%fused_computation.3 | convolution fusion | flops 1074266112 | bytes 5767168 | tf_op jit(solution)/shard_map/dot_general | solution.py:182
  (104 shorter events, 14.9 us)
Async XLA Ops:
  7.2 90.4 %copy-start.3 = (bf16[1,256,2048]{2,1,0:T(8,128)(2,1)S(1)}, bf16[1,256,2048]{2,1,0:T(8,128)(2,1)}, u32[]{:S(2)}) copy-start(bf16[1,256,2048]{2,1,0:T(8,128)(2,1)} %param.11) | copy-start | bytes 3145732
  7.2 90.7 %copy-start.10 = (bf16[1,32,1024]{2,1,0:T(8,128)(2,1)S(1)}, bf16[1,32,1024]{2,1,0:T(8,128)(2,1)}, u32[]{:S(2)}) copy-start(bf16[1,32,1024]{2,1,0:T(8,128)(2,1)} %param.13) | copy-start | bytes 196612
  7.2 97.7 %copy-start.17 = (s32[4]{0:T(128)S(1)}, s32[4]{0:T(128)}, u32[]{:S(2)}) copy-start(s32[4]{0:T(128)} %param.14) | copy-start | bytes 52
  7.2 119.7 %all-gather.7.cloned.1.call-start = ((), (), s32[]{:S(2)}) async-start(), calls=%async_computation | async-start | bytes 9437184 | tf_op jit(solution)/shard_map/all_gather | solution.py:117
  7.9 161.0 %all-gather.9.cloned.1.call-start = ((), (), s32[]{:S(2)}) async-start(), calls=%async_computation.1 | async-start | bytes 4718592 | tf_op jit(solution)/shard_map/all_gather | solution.py:184
  90.2 36.5 %collective-permute-start = (s32[256]{0:T(256)S(1)}, s32[256]{0:T(256)S(1)}, u32[]{:S(2)}, u32[]{:S(2)}) collective-permute-start(s32[256]{0:T(256)S(1)} %get-tuple-element.203), channel_id=1, source_target_pairs={{0,1},{1,2},{2,3},{3,4},{4,5},{5,6},{6,7},{8,9},{9,10},{10,11},{11... | collective-permute-start | bytes 3080 | tf_op jit(solution)/shard_map/ppermute | solution.py:32
  94.1 32.7 %collective-permute-start.2 = (s32[256]{0:T(256)S(1)}, s32[256]{0:T(256)S(1)}, u32[]{:S(2)}, u32[]{:S(2)}) collective-permute-start(s32[256]{0:T(256)S(1)} %get-tuple-element.203), channel_id=1, source_target_pairs={{0,2},{1,3},{2,4},{3,5},{4,6},{5,7},{8,10},{9,11},{10,12},{11,13},... | collective-permute-start | bytes 3080 | tf_op jit(solution)/shard_map/ppermute | solution.py:32
  97.6 29.1 %copy-start.16 = (bf16[2048]{0:T(1024)(128)(2,1)S(1)}, bf16[2048]{0:T(1024)(128)(2,1)}, u32[]{:S(2)}) copy-start(bf16[2048]{0:T(1024)(128)(2,1)} %param.15) | copy-start | bytes 12292
  97.6 29.1 %copy-start.18 = (bf16[128]{0:T(256)(128)(2,1)S(1)}, bf16[128]{0:T(256)(128)(2,1)}, u32[]{:S(2)}) copy-start(bf16[128]{0:T(256)(128)(2,1)} %param.17) | copy-start | bytes 772
  97.6 29.1 %copy-start.19 = (bf16[128]{0:T(256)(128)(2,1)S(1)}, bf16[128]{0:T(256)(128)(2,1)}, u32[]{:S(2)}) copy-start(bf16[128]{0:T(256)(128)(2,1)} %param.16) | copy-start | bytes 772
  132.8 1.4 copy-start.1
  135.0 6.4 %copy-start.2 = (f32[256,2048]{1,0:T(8,128)S(1)}, f32[256,2048]{1,0:T(8,128)}, u32[]{:S(2)}) copy-start(f32[256,2048]{1,0:T(8,128)} %copy-done.1) | copy-start | bytes 6291460
  136.3 17.8 %collective-permute-start.3 = (bf16[256,1024]{1,0:T(8,128)(2,1)}, bf16[256,1024]{1,0:T(8,128)(2,1)}, u32[]{:S(2)}, u32[]{:S(2)}) collective-permute-start(bf16[256,1024]{1,0:T(8,128)(2,1)} %pad_maximum_fusion.1), channel_id=1, source_target_pairs={{0,2},{1,3},{2,4},{3,5},{4,6},{5,7},{8,10},{9,11},{10,12},{11,13},... | collective-permute-start | bytes 1572872 | tf_op jit(solution)/shard_map/ppermute | solution.py:32
  138.4 19.5 %collective-permute-start.1 = (bf16[256,1024]{1,0:T(8,128)(2,1)}, bf16[256,1024]{1,0:T(8,128)(2,1)}, u32[]{:S(2)}, u32[]{:S(2)}) collective-permute-start(bf16[256,1024]{1,0:T(8,128)(2,1)} %pad_maximum_fusion.1), channel_id=1, source_target_pairs={{0,1},{1,2},{2,3},{3,4},{4,5},{5,6},{6,7},{8,9},{9,10},{10,11},{11... | collective-permute-start | bytes 1572872 | tf_op jit(solution)/shard_map/ppermute | solution.py:32
  143.2 2.4 %copy-start.4 = (bf16[256,512]{0,1:T(8,128)(2,1)S(1)}, bf16[256,512]{0,1:T(8,128)(2,1)}, u32[]{:S(2)}) copy-start(bf16[256,512]{0,1:T(8,128)(2,1)} %get-tuple-element.193) | copy-start | bytes 786436
  143.8 2.3 %copy-start.5 = (pred[256,256]{0,1:T(8,128)(4,1)S(1)}, pred[256,256]{0,1:T(8,128)(4,1)}, u32[]{:S(2)}) copy-start(pred[256,256]{0,1:T(8,128)(4,1)} %fusion.62) | copy-start | bytes 196612
  163.6 1.1 copy-start.13
  163.6 1.1 copy-start.14
  163.6 1.1 copy-start.15
  163.6 1.2 copy-start.9
  164.8 1.6 copy-start
  164.8 1.6 copy-start.6
  164.8 1.6 copy-start.7
  166.4 0.7 copy-start.11
  166.4 0.7 copy-start.12
  167.1 1.0 copy-start.8
Sparse Core Ops, SparseCore 0:
  9.6 84.7 all-gather.6
  96.2 49.5 all-gather.8
where the time goes:
time: 182 us; the launch traced here: 180 us
  local copies, waits for them, and re-layouts  42 us (23%)
  loops' own time  41 us (23%)
  blocking collectives  35.4 us (19%)
  between operations  16.6 us (9%)
  matrix products  16.4 us (9%)
  other arithmetic  15.3 us (8%)
  starting transfers between devices  11 us (6%)
  waiting for transfers between devices  2.6 us (1%)
    another operation x1, loops' own time, entering(): return lax.fori_loop(0, length, hop, start)  41 us
    dynamic_slice x32, local copies, waits for them, and re-layouts, hop(): new = combine(before, jax.tree.map(lambda part: part[k], everything))  19.1 us
    all_gather x1, blocking collectives, per_device(): piece = lax.all_gather(own_rows, 'tok', axis=0, tiled=True)  19 us
    ppermute x4, starting transfers between devices, shifted(): return lax.ppermute(block, axis, route)  10.9 us
    unnamed x52, local copies, waits for them, and re-layouts  9.71 us
    all_gather x1, blocking collectives, entering(): everything = jax.tree.map(lambda part: lax.all_gather(part, axis), x)  9.36 us
    all_gather x1, blocking collectives, per_device(): owners = lax.all_gather(prefix_kv[0], 'grp', axis=0, tiled=True)  6.97 us
    dot_general x1, matrix products, per_device(): jnp.dot(columns, lax.all_gather(w_qkv, 'tok', axis=0, tiled=True), prefer...  5.84 us
  transfers between devices with their start and end apart: 6, of which 1 were waited for; matrix products, arithmetic and copies ran while one was open for 37% of the time, Pallas kernels for 0%

commit v1 on v0

v1 whole, which is shorter than its diff:
```python
import functools
import math

import jax
import jax.numpy as jnp
import numpy as np
from jax import lax
from jax.experimental import pallas as pl
from jax.experimental.pallas import tpu as pltpu
from jax.sharding import PartitionSpec as P

MESH = pl.DeviceIdType.MESH
epsilon = 1e-06
theta_base = 1000000.0
floor_score = -1e30
REACH = 2
BLOCK = 256


class Gather:
    def __init__(self, own, buf, send, recv, nz, split):
        self.own, self.buf, self.send, self.recv = own, buf, send, recv
        self.nz, self.split = nz, split
        g, t = lax.axis_index("grp"), lax.axis_index("tok")
        self.g, self.t = g, t
        self.z, self.c = t // 2, t % 2
        self.gx = g + 1 - 2 * (g % 2)
        self.gy = (g + 2) % 4
        self.gd = (self.gx + 2) % 4
        width = buf.shape[2]
        if split:
            q = width // 4
            self.ranges = (
                (self.g * q, q),
                (self.gx * q, q),
                (self.gy * q, q),
                (self.gd * q, q // 2),
                (self.gd * q + q // 2, q // 2),
            )
        else:
            self.ranges = ((0, width),)

    def at(self, ref, lo, width):
        if isinstance(lo, int):
            return ref.at[:, pl.ds(lo, width)]
        return ref.at[:, pl.ds(pl.multiple_of(lo, 128), width)]

    def copy(self, zz, core, lo, width, s, r, dev, own=False):
        place = self.at(self.buf.at[zz * 2 + core], lo, width)
        src = self.at(self.own, lo, width) if own else place
        return pltpu.make_async_remote_copy(
            src_ref=src,
            dst_ref=place,
            send_sem=self.send.at[s, zz],
            recv_sem=self.recv.at[r, zz],
            device_id=dev,
            device_id_type=MESH,
        )

    def dev_z(self, zz):
        return (self.g, zz * 2 + self.c)

    @property
    def sibling(self):
        return (self.g, self.z * 2 + 1 - self.c)

    def up(self, zz, own=False):
        return self.copy(zz, self.c, *self.ranges[0], 0, 0, self.dev_z(self.z + 1), own)

    def down(self, zz, own=False):
        return self.copy(zz, self.c, *self.ranges[0], 1 if own else 0, 0, self.dev_z(self.z - 1), own)

    def to_x(self, zz):
        return self.copy(zz, self.c, *self.ranges[0], 1, 1, (self.gx, self.t))

    def to_y(self, zz):
        return self.copy(zz, self.c, *self.ranges[0], 2, 2, (self.gy, self.t))

    def on_y(self, zz):
        lo, width = self.ranges[1]
        return self.copy(zz, self.c, lo, width // 2, 3, 3, (self.gy, self.t))

    def on_x(self, zz):
        lo, width = self.ranges[2]
        return self.copy(zz, self.c, lo + width // 2, width // 2, 4, 4, (self.gx, self.t))

    def across(self, zz, kind):
        return self.copy(zz, self.c, *self.ranges[kind], 5 + kind, 5 + kind, self.sibling)

    def across_own(self):
        return self.copy(self.z, self.c, 0, self.buf.shape[2], 5, 5, self.sibling, True)

    def wait_recv(self, zz, kind):
        self.copy(zz, self.c, *self.ranges[kind], kind, kind, self.sibling).wait_recv()

    def start(self):
        @pl.when(self.z + 1 < self.nz)
        def _():
            self.up(self.z, True).start()

        @pl.when(self.z > 0)
        def _():
            self.down(self.z, True).start()

        self.across_own().start()

    def arrive(self, zz):
        self.wait_recv(zz, 0)

        @pl.when((zz < self.z) & (self.z + 1 < self.nz))
        def _():
            self.up(zz).start()

        @pl.when((zz > self.z) & (self.z > 0))
        def _():
            self.down(zz).start()

        if self.split:
            self.to_x(zz).start()
            self.to_y(zz).start()
        self.across(zz, 0).start()

    def plane(self, zz):
        self.wait_recv(zz, 1)
        self.on_y(zz).start()
        self.across(zz, 1).start()
        self.wait_recv(zz, 2)
        self.on_x(zz).start()
        self.across(zz, 2).start()

    def diagonal(self, zz):
        for kind in (3, 4):
            self.wait_recv(zz, kind)
            self.across(zz, kind).start()

    def both(self, s, what):
        @pl.when((s >= 1) & (self.z - s >= 0))
        def _():
            what(self.z - s)

        @pl.when((s >= 1) & (self.z + s < self.nz))
        def _():
            what(self.z + s)

    def steps(self, first, last):
        def step(s, carry):
            self.both(s, self.arrive)
            if self.split:
                self.both(s - 1, self.plane)
                self.both(s - 2, self.diagonal)
            return carry

        lax.fori_loop(first, last, step, 0)

    def finish(self):
        def settle(zz, carry):
            @pl.when(zz != self.z)
            def _():
                for kind in range(len(self.ranges)):
                    lo, width = self.ranges[kind]
                    self.copy(
                        zz, 1 - self.c, lo, width, 5 + kind, 5 + kind, self.sibling
                    ).wait_recv()

            @pl.when(zz == self.z)
            def _():
                self.copy(
                    zz, 1 - self.c, 0, self.buf.shape[2], 5, 5, self.sibling
                ).wait_recv()

            return carry

        lax.fori_loop(0, self.nz, settle, 0)

    def sent(self):
        def settle(zz, carry):
            @pl.when(zz != self.z)
            def _():
                @pl.when((zz < self.z) & (self.z + 1 < self.nz))
                def _():
                    self.up(zz).wait_send()

                @pl.when((zz > self.z) & (self.z > 0))
                def _():
                    self.down(zz).wait_send()

                if self.split:
                    self.to_x(zz).wait_send()
                    self.to_y(zz).wait_send()
                    self.on_y(zz).wait_send()
                    self.on_x(zz).wait_send()
                for kind in range(len(self.ranges)):
                    self.across(zz, kind).wait_send()

            return carry

        lax.fori_loop(0, self.nz, settle, 0)

        @pl.when(self.z + 1 < self.nz)
        def _():
            self.up(self.z, True).wait_send()

        @pl.when(self.z > 0)
        def _():
            self.down(self.z, True).wait_send()

        self.across_own().wait_send()


def kernel(
    nt, ng,
    owner_ref, freq_ref, hidden_ref, ids_ref, prefix_ref, ngain_ref, qgain_ref, kgain_ref,
    wq_ref, wo_ref,
    out_ref, key_ref, value_ref,
    wq, wo, pall, psel, kv, ids_buf, normed, queries, attended, bias,
    q_send, q_recv, o_send, o_recv, p_send, p_recv, pa_send, pa_recv,
    id_send, id_recv, kv_send, kv_recv,
):
    g, t = lax.axis_index("grp"), lax.axis_index("tok")
    nz = nt // 2
    z, c = t // 2, t % 2
    rows = hidden_ref.shape[1]
    head = qgain_ref.shape[1]
    kvw = key_ref.shape[2]
    kv_heads = kvw // head
    qkvw = wq.shape[2]
    qw = qkvw - 2 * kvw
    ratio = (qw // head) // kv_heads
    depth = wq.shape[0] * wq.shape[1]

    barrier = pltpu.get_barrier_semaphore()

    def greet_tok(k, carry):
        pl.semaphore_signal(
            barrier, inc=1, device_id=(g, (t + k) % nt), device_id_type=MESH
        )
        return carry

    lax.fori_loop(1, nt, greet_tok, 0)
    for k in range(1, ng):
        pl.semaphore_signal(
            barrier, inc=1, device_id=((g + k) % ng, t), device_id_type=MESH
        )
    ids = ids_ref[...]
    ids_buf[0] = jnp.broadcast_to(ids, ids_buf.shape[1:])
    for back in range(1, REACH + 1):
        @pl.when(t < back)
        def _():
            ids_buf[back] = jnp.full(ids_buf.shape[1:], -1, jnp.int32)
            kv[back] = jnp.zeros(kv.shape[1:], kv.dtype)
    pl.semaphore_wait(barrier, nt - 1 + ng - 1)

    qg = Gather(wq_ref, wq, q_send, q_recv, nz, True)
    og = Gather(wo_ref, wo, o_send, o_recv, nz, True)
    pg = Gather(psel.at[t], psel, p_send, p_recv, nz, False)

    def id_copy(back):
        return pltpu.make_async_remote_copy(
            src_ref=ids_buf.at[0], dst_ref=ids_buf.at[back],
            send_sem=id_send.at[back], recv_sem=id_recv.at[back],
            device_id=(g, (t + back) % nt), device_id_type=MESH,
        )

    for back in range(1, REACH + 1):
        @pl.when(t + back < nt)
        def _():
            id_copy(back).start()

    def prefix_copy(k):
        return pltpu.make_async_remote_copy(
            src_ref=prefix_ref.at[0], dst_ref=pall.at[g],
            send_sem=pa_send.at[k], recv_sem=pa_recv.at[k],
            device_id=((g + k) % ng, t), device_id_type=MESH,
        )

    def prefix_got(k):
        return pltpu.make_async_remote_copy(
            src_ref=prefix_ref.at[0], dst_ref=pall.at[(g + ng - k) % ng],
            send_sem=pa_send.at[k], recv_sem=pa_recv.at[k],
            device_id=((g + k) % ng, t), device_id_type=MESH,
        )

    for k in range(1, ng):
        prefix_copy(k).start()
    qg.start()

    wq[t] = wq_ref[...]
    wo[t] = wo_ref[...]
    pall[g] = prefix_ref[0]

    def norm_rows(i, carry):
        at = pl.ds(pl.multiple_of(i * 64, 64), 64)
        x = hidden_ref[0, at, :].astype(jnp.float32)
        x = x * lax.rsqrt(jnp.mean(x * x, axis=-1, keepdims=True) + epsilon)
        normed[at, :] = (x * ngain_ref[...].astype(jnp.float32)).astype(jnp.bfloat16)
        return carry

    lax.fori_loop(0, rows // 64, norm_rows, 0)

    for k in range(1, ng):
        prefix_got(k).wait_recv()
    psel[t] = pall[owner_ref[g]]
    pg.start()

    for back in range(1, REACH + 1):
        @pl.when(t >= back)
        def _():
            id_copy(back).wait_recv()
    column = jnp.transpose(
        jnp.broadcast_to(ids.astype(jnp.float32), (128, rows)), (1, 0)
    )[:, :1]
    here = lax.broadcasted_iota(jnp.int32, (rows, rows), 0)
    there = lax.broadcasted_iota(jnp.int32, (rows, rows), 1)
    count = jnp.zeros((rows, 1), jnp.float32)
    for back in range(REACH + 1):
        allowed = column == ids_buf[back, 0:1, :].astype(jnp.float32)
        if back == 0:
            allowed = allowed & (there <= here)
        count += jnp.sum(jnp.where(allowed, 1.0, 0.0), axis=-1, keepdims=True)
        bias[back] = jnp.where(allowed, 0.0, floor_score)
    prefix_len = psel.shape[0] * psel.shape[1]
    position = count + (prefix_len - 1.0)
    angles = position * freq_ref[...]
    cosine = jnp.cos(angles)
    lane = lax.broadcasted_iota(jnp.int32, (rows, head), 1)
    sine = jnp.sin(angles)
    sine = jnp.where(lane < head // 2, -sine, sine)

    def arrived(s, carry):
        qg.both(s, qg.arrive)
        pg.both(s, pg.arrive)
        qg.both(s - 1, qg.plane)
        qg.both(s - 2, qg.diagonal)
        return carry

    lax.fori_loop(1, nz, arrived, 0)
    og.start()
    qg.steps(nz, nz + 2)
    qg.finish()

    def project(j):
        at = pl.ds(pl.multiple_of(j * BLOCK, BLOCK), BLOCK)
        w = wq[:, :, at].reshape(depth, BLOCK)
        return jnp.dot(normed[...], w, preferred_element_type=jnp.float32)

    def turned(block, gain):
        parts = []
        for i in range(BLOCK // head):
            a = block[:, i * head:(i + 1) * head]
            a = a * lax.rsqrt(jnp.mean(a * a, axis=-1, keepdims=True) + epsilon)
            a = a * gain
            a = a * cosine + pltpu.roll(a, head // 2, 1) * sine
            parts.append(a.astype(jnp.bfloat16))
        return jnp.concatenate(parts, axis=1)

    def key_block(j, carry):
        at = pl.ds(pl.multiple_of(j * BLOCK, BLOCK), BLOCK)
        made = turned(project(qw // BLOCK + j), kgain_ref[...].astype(jnp.float32))
        kv[0, :, at] = made
        key_ref[0, :, at] = made
        return carry

    def value_block(j, carry):
        made = project((qw + kvw) // BLOCK + j).astype(jnp.bfloat16)
        kv[0, :, pl.ds(pl.multiple_of(kvw + j * BLOCK, BLOCK), BLOCK)] = made
        value_ref[0, :, pl.ds(pl.multiple_of(j * BLOCK, BLOCK), BLOCK)] = made
        return carry

    def query_block(j, carry):
        at = pl.ds(pl.multiple_of(j * BLOCK, BLOCK), BLOCK)
        queries[:, at] = turned(project(j), qgain_ref[...].astype(jnp.float32))
        return carry

    lax.fori_loop(0, kvw // BLOCK, key_block, 0)
    lax.fori_loop(0, kvw // BLOCK, value_block, 0)

    def kv_copy(src, dst, dev):
        return pltpu.make_async_remote_copy(
            src_ref=kv.at[src], dst_ref=kv.at[dst],
            send_sem=kv_send.at[dst], recv_sem=kv_recv.at[dst],
            device_id=(g, dev), device_id_type=MESH,
        )

    to_next = kv_copy(0, 2, (t + 2) % nt)
    beside = kv_copy(0, 1, z * 2 + 1 - c)
    passed_on = kv_copy(2, 1, z * 2 + 1 - c)

    @pl.when(t + 2 < nt)
    def _():
        to_next.start()

    @pl.when(c == 0)
    def _():
        beside.start()

    lax.fori_loop(0, qw // BLOCK, query_block, 0)
    pg.finish()

    @pl.when(t >= 2)
    def _():
        to_next.wait_recv()

    @pl.when((c == 1) & (z > 0))
    def _():
        passed_on.start()

    @pl.when(t >= 1)
    def _():
        beside.wait_recv()

    factor = head ** (-0.5) * math.log2(math.e)
    dims = (((1,), (1,)), ((), ()))

    def attend(h, carry):
        kat = pl.ds(pl.multiple_of(h * head, head), head)
        vat = pl.ds(pl.multiple_of(kvw + h * head, head), head)
        q = jnp.concatenate(
            [
                queries[:, pl.ds(pl.multiple_of((h * ratio + r) * head, head), head)]
                for r in range(ratio)
            ],
            axis=0,
        )
        keys = [psel[:, :, kat].reshape(prefix_len, head)]
        values = [psel[:, :, vat].reshape(prefix_len, head)]
        for back in range(REACH + 1):
            keys.append(kv[back, :, kat])
            values.append(kv[back, :, vat])
        scores = []
        for i, k in enumerate(keys):
            s = lax.dot_general(q, k, dims, preferred_element_type=jnp.float32)
            if i:
                s = (s.reshape(ratio, rows, rows) + bias[i - 1][None]).reshape(ratio * rows, rows)
            scores.append(s)
        top = functools.reduce(
            jnp.maximum, [jnp.max(s, axis=-1, keepdims=True) for s in scores]
        )
        total, mixed = 0.0, 0.0
        for s, v in zip(scores, values):
            p = jnp.exp2((s - top) * factor)
            total += jnp.sum(p, axis=-1, keepdims=True)
            mixed += jnp.dot(p.astype(jnp.bfloat16), v, preferred_element_type=jnp.float32)
        mixed = (mixed / total).astype(jnp.bfloat16)
        for r in range(ratio):
            attended[:, pl.ds(pl.multiple_of((h * ratio + r) * head, head), head)] = mixed[
                r * rows:(r + 1) * rows
            ]
        og.steps(1 + h * per, jnp.minimum(1 + (h + 1) * per, nz + 2))
        return carry

    per = -(-(nz + 1) // kv_heads)
    lax.fori_loop(0, kv_heads, attend, 0)
    og.finish()

    def out_block(j, carry):
        at = pl.ds(pl.multiple_of(j * BLOCK, BLOCK), BLOCK)
        w = wo[:, :, at].reshape(qw, BLOCK)
        out_ref[0, :, at] = jnp.dot(
            attended[...], w, preferred_element_type=jnp.float32
        ).astype(jnp.bfloat16)
        return carry

    lax.fori_loop(0, out_ref.shape[2] // BLOCK, out_block, 0)

    for one in (qg, og, pg):
        one.sent()
    for k in range(1, ng):
        prefix_copy(k).wait_send()
    for back in range(1, REACH + 1):
        @pl.when(t + back < nt)
        def _():
            id_copy(back).wait_send()

    @pl.when(t + 2 < nt)
    def _():
        to_next.wait_send()

    @pl.when(c == 0)
    def _():
        beside.wait_send()

    @pl.when((c == 1) & (z > 0))
    def _():
        passed_on.wait_send()


def per_device(
    nt, ng,
    hidden_in, doc_ids, prefix_kv, prefix_owner, norm_gain, query_gain, key_norm_gain, w_qkv, w_out
):
    rows, width = hidden_in.shape[1:]
    head = query_gain.shape[0]
    kvw = prefix_kv.shape[2] // 2
    pre = prefix_kv.shape[1]
    qkvw = w_qkv.shape[1]
    qw = qkvw - 2 * kvw
    nz = nt // 2
    half = head // 2
    freqs = np.float32(theta_base) ** (-np.arange(half, dtype=np.float32) / np.float32(half))
    freqs = np.concatenate([freqs, freqs]).astype(np.float32)[None]
    bf = jnp.bfloat16
    vm = pl.BlockSpec(memory_space=pltpu.VMEM)
    dma = pltpu.SemaphoreType.DMA
    return pl.pallas_call(
        functools.partial(kernel, nt, ng),
        out_shape=(
            jax.ShapeDtypeStruct((1, rows, w_out.shape[1]), bf),
            jax.ShapeDtypeStruct((1, rows, kvw), bf),
            jax.ShapeDtypeStruct((1, rows, kvw), bf),
        ),
        in_specs=[pl.BlockSpec(memory_space=pltpu.SMEM)] + [vm] * 9,
        out_specs=(vm, vm, vm),
        scratch_shapes=[
            pltpu.VMEM((nt,) + w_qkv.shape, bf),
            pltpu.VMEM((nt,) + w_out.shape, bf),
            pltpu.VMEM((ng, pre, 2 * kvw), bf),
            pltpu.VMEM((nt, pre, 2 * kvw), bf),
            pltpu.VMEM((REACH + 1, rows, 2 * kvw), bf),
            pltpu.VMEM((REACH + 1, 8, rows), jnp.int32),
            pltpu.VMEM((rows, width), bf),
            pltpu.VMEM((rows, qw), bf),
            pltpu.VMEM((rows, qw), bf),
            pltpu.VMEM((REACH + 1, rows, rows), jnp.float32),
            dma((10, nz)), dma((10, nz)),
            dma((10, nz)), dma((10, nz)),
            dma((10, nz)), dma((10, nz)),
            dma((ng,)), dma((ng,)),
            dma((REACH + 1,)), dma((REACH + 1,)),
            dma((REACH + 1,)), dma((REACH + 1,)),
        ],
        compiler_params=pltpu.CompilerParams(
            collective_id=0, has_side_effects=True, vmem_limit_bytes=56 * 1024 * 1024
        ),
    )(
        prefix_owner, jnp.asarray(freqs), hidden_in, doc_ids, prefix_kv,
        norm_gain[None], query_gain[None], key_norm_gain[None], w_qkv, w_out,
    )


def solution(mesh):
    return jax.shard_map(
        functools.partial(per_device, mesh.shape["tok"], mesh.shape["grp"]),
        mesh=mesh,
        in_specs=(
            P("grp", "tok", None),
            P("grp", "tok"),
            P("grp", "tok", None),
            P(),
            P(),
            P(),
            P(),
            P("tok", None),
            P("tok", None),
        ),
        out_specs=(P("grp", "tok", None), P("grp", "tok", None), P("grp", "tok", None)),
        check_vma=False,
    )
```

time: 182 us -> 92.4 us (0.51)
  the two profiles are of different devices: /device:TPU:1 before, /device:TPU:0 now
where the time goes in v1:
time: 92.4 us; the launch traced here: 92.1 us
  Pallas kernels  86.1 us (93%)
  local copies, waits for them, and re-layouts  5.39 us (6%)
    pallas_call x1, Pallas kernels, per_device(): pl.pallas_call(functools.partial(kernel, nt, ng), out_shape=(jax.ShapeDty...  86.1 us
    unnamed x7, local copies, waits for them, and re-layouts  4.1 us

profile of v1, /device:TPU:0, one launch (start us, length us, event | category | flops | bytes accessed | tf_op | source)
XLA Modules:
  0.0 92.1 jit_solution(4072160545095447825)
XLA Ops:
  0.6 1.3 %broadcast_in_dim.9.ngain_ref = bf16[1,2048]{1,0:T(2,128)(2,1)} reshape(bf16[2048]{0:T(1024)(128)(2,1)} %param.14) | data formatting | bytes 8192 | tf_op jit(solution)/shard_map/broadcast_in_dim | solution.py:536
  1.9 86.1 %shard_map.121 = (bf16[1,256,2048]{2,1,0:T(8,128)(2,1)}, bf16[1,256,512]{2,1,0:T(8,128)(2,1)}, bf16[1,256,512]{2,1,0:T(8,128)(2,1)}) custom-call(s32[4]{0:T(128)} %owner_ref.1, f32[1,128]{1,0:T(1,128)} %constant.2.clone.freq_ref, bf16[1,256,2048]{2,1,0:T(8,128)(2,1)} %hidden_ref.1, s32[1,256]{1,0:T(1,128)} %ids_ref.1, bf16[1,32,1024]{2,1,0:T(8,128)(2,1)} %prefix_ref.1, ...), custom_call_target="tpu_custom_call" | custom-call | tf_op jit(solution)/shard_map/pallas_call | solution.py:504
  88.0 0.0 copy-start.1
  88.0 2.3 %copy.16 = bf16[1,256,2048]{2,1,0:T(8,128)(2,1)} copy(bf16[1,256,2048]{2,1,0:T(8,128)(2,1)} %get-tuple-element.6) | data formatting | bytes 2097152
  90.4 0.0 copy-done.1
  90.4 0.0 copy-start
  90.4 0.7 copy.17
  91.1 0.3 copy-done
  91.4 0.7 copy.18
Async XLA Ops:
  88.0 2.4 %copy-start.1 = (bf16[1,256,512]{2,1,0:T(8,128)(2,1)S(1)}, bf16[1,256,512]{2,1,0:T(8,128)(2,1)}, u32[]{:S(2)}) copy-start(bf16[1,256,512]{2,1,0:T(8,128)(2,1)} %get-tuple-element.7) | copy-start | bytes 786436
  90.4 1.0 %copy-start = (bf16[1,256,512]{2,1,0:T(8,128)(2,1)S(1)}, bf16[1,256,512]{2,1,0:T(8,128)(2,1)}, u32[]{:S(2)}) copy-start(bf16[1,256,512]{2,1,0:T(8,128)(2,1)} %get-tuple-element.8) | copy-start | bytes 786436

commit v2 on v1

--- a/solution.py
+++ b/solution.py
@@ -18,7 +18,7 @@
 
 
 class Gather:
-    def __init__(self, own, buf, send, recv, nz, split):
+    def __init__(self, own, buf, send, recv, nz, split, base=0, width=None):
         self.own, self.buf, self.send, self.recv = own, buf, send, recv
         self.nz, self.split = nz, split
         g, t = lax.axis_index("grp"), lax.axis_index("tok")
@@ -27,18 +27,19 @@
         self.gx = g + 1 - 2 * (g % 2)
         self.gy = (g + 2) % 4
         self.gd = (self.gx + 2) % 4
-        width = buf.shape[2]
+        width = buf.shape[2] if width is None else width
+        self.whole = (base, width)
         if split:
             q = width // 4
             self.ranges = (
-                (self.g * q, q),
-                (self.gx * q, q),
-                (self.gy * q, q),
-                (self.gd * q, q // 2),
-                (self.gd * q + q // 2, q // 2),
+                (base + self.g * q, q),
+                (base + self.gx * q, q),
+                (base + self.gy * q, q),
+                (base + self.gd * q, q // 2),
+                (base + self.gd * q + q // 2, q // 2),
             )
         else:
-            self.ranges = ((0, width),)
+            self.ranges = (self.whole,)
 
     def at(self, ref, lo, width):
         if isinstance(lo, int):
@@ -88,7 +89,7 @@
         return self.copy(zz, self.c, *self.ranges[kind], 5 + kind, 5 + kind, self.sibling)
 
     def across_own(self):
-        return self.copy(self.z, self.c, 0, self.buf.shape[2], 5, 5, self.sibling, True)
+        return self.copy(self.z, self.c, *self.whole, 5, 5, self.sibling, True)
 
     def wait_recv(self, zz, kind):
         self.copy(zz, self.c, *self.ranges[kind], kind, kind, self.sibling).wait_recv()
@@ -115,10 +116,11 @@
         def _():
             self.down(zz).start()
 
-        if self.split:
-            self.to_x(zz).start()
-            self.to_y(zz).start()
         self.across(zz, 0).start()
+
+    def spread(self, zz):
+        self.to_x(zz).start()
+        self.to_y(zz).start()
 
     def plane(self, zz):
         self.wait_recv(zz, 1)
@@ -142,15 +144,9 @@
         def _():
             what(self.z + s)
 
-    def steps(self, first, last):
-        def step(s, carry):
-            self.both(s, self.arrive)
-            if self.split:
-                self.both(s - 1, self.plane)
-                self.both(s - 2, self.diagonal)
-            return carry
-
-        lax.fori_loop(first, last, step, 0)
+    def step(self, s):
+        self.both(s - 1, self.plane)
+        self.both(s - 2, self.diagonal)
 
     def finish(self):
         def settle(zz, carry):
@@ -164,9 +160,7 @@
 
             @pl.when(zz == self.z)
             def _():
-                self.copy(
-                    zz, 1 - self.c, 0, self.buf.shape[2], 5, 5, self.sibling
-                ).wait_recv()
+                self.copy(zz, 1 - self.c, *self.whole, 5, 5, self.sibling).wait_recv()
 
             return carry
 
@@ -213,6 +207,7 @@
     wq_ref, wo_ref,
     out_ref, key_ref, value_ref,
     wq, wo, pall, psel, kv, ids_buf, normed, queries, attended, bias,
+    k_send, k_recv,
     q_send, q_recv, o_send, o_recv, p_send, p_recv, pa_send, pa_recv,
     id_send, id_recv, kv_send, kv_recv,
 ):
@@ -250,7 +245,8 @@
             kv[back] = jnp.zeros(kv.shape[1:], kv.dtype)
     pl.semaphore_wait(barrier, nt - 1 + ng - 1)
 
-    qg = Gather(wq_ref, wq, q_send, q_recv, nz, True)
+    kg = Gather(wq_ref, wq, k_send, k_recv, nz, True, qw, 2 * kvw)
+    qg = Gather(wq_ref, wq, q_send, q_recv, nz, True, 0, qw)
     og = Gather(wo_ref, wo, o_send, o_recv, nz, True)
     pg = Gather(psel.at[t], psel, p_send, p_recv, nz, False)
 
@@ -282,7 +278,7 @@
 
     for k in range(1, ng):
         prefix_copy(k).start()
-    qg.start()
+    kg.start()
 
     wq[t] = wq_ref[...]
     wo[t] = wo_ref[...]
@@ -300,7 +296,6 @@
     for k in range(1, ng):
         prefix_got(k).wait_recv()
     psel[t] = pall[owner_ref[g]]
-    pg.start()
 
     for back in range(1, REACH + 1):
         @pl.when(t >= back)
@@ -326,17 +321,25 @@
     sine = jnp.sin(angles)
     sine = jnp.where(lane < head // 2, -sine, sine)
 
-    def arrived(s, carry):
+    def first(s, carry):
+        kg.both(s, kg.arrive)
+        kg.both(s, kg.spread)
+        kg.step(s)
+        return carry
+
+    lax.fori_loop(1, nz, first, 0)
+    qg.start()
+    pg.start()
+
+    def second(s, carry):
         qg.both(s, qg.arrive)
-        pg.both(s, pg.arrive)
-        qg.both(s - 1, qg.plane)
-        qg.both(s - 2, qg.diagonal)
-        return carry
-
-    lax.fori_loop(1, nz, arrived, 0)
+        kg.step(nz - 1 + s)
+        qg.both(s, qg.spread)
+        return carry
+
+    lax.fori_loop(1, nz, second, 0)
     og.start()
-    qg.steps(nz, nz + 2)
-    qg.finish()
+    kg.finish()
 
     def project(j):
         at = pl.ds(pl.multiple_of(j * BLOCK, BLOCK), BLOCK)
@@ -393,6 +396,16 @@
     def _():
         beside.start()
 
+    def third(s, carry):
+        pg.both(s, pg.arrive)
+        og.both(s, og.arrive)
+        qg.step(s + 1)
+        og.both(s, og.spread)
+        return carry
+
+    lax.fori_loop(1, nz, third, 0)
+    qg.step(nz + 1)
+    qg.finish()
     lax.fori_loop(0, qw // BLOCK, query_block, 0)
     pg.finish()
 
@@ -445,10 +458,15 @@
             attended[:, pl.ds(pl.multiple_of((h * ratio + r) * head, head), head)] = mixed[
                 r * rows:(r + 1) * rows
             ]
-        og.steps(1 + h * per, jnp.minimum(1 + (h + 1) * per, nz + 2))
-        return carry
-
-    per = -(-(nz + 1) // kv_heads)
+
+        def fourth(s, carry):
+            og.step(s)
+            return carry
+
+        lax.fori_loop(2 + h * per, jnp.minimum(2 + (h + 1) * per, nz + 2), fourth, 0)
+        return carry
+
+    per = -(-nz // kv_heads)
     lax.fori_loop(0, kv_heads, attend, 0)
     og.finish()
 
@@ -462,7 +480,7 @@
 
     lax.fori_loop(0, out_ref.shape[2] // BLOCK, out_block, 0)
 
-    for one in (qg, og, pg):
+    for one in (kg, qg, og, pg):
         one.sent()
     for k in range(1, ng):
         prefix_copy(k).wait_send()
@@ -524,6 +542,7 @@
             dma((10, nz)), dma((10, nz)),
             dma((10, nz)), dma((10, nz)),
             dma((10, nz)), dma((10, nz)),
+            dma((10, nz)), dma((10, nz)),
             dma((ng,)), dma((ng,)),
             dma((REACH + 1,)), dma((REACH + 1,)),
             dma((REACH + 1,)), dma((REACH + 1,)),

time: 92.4 us -> 91.4 us (0.989)
  the two profiles are of different devices: /device:TPU:0 before, /device:TPU:25 now
where the time goes in v2:
time: 91.4 us; the launch traced here: 91.2 us
  Pallas kernels  85.1 us (93%)
  local copies, waits for them, and re-layouts  5.39 us (6%)
    pallas_call x1, Pallas kernels, per_device(): pl.pallas_call(functools.partial(kernel, nt, ng), out_shape=(jax.ShapeDty...  85.1 us
    unnamed x7, local copies, waits for them, and re-layouts  4.1 us

profile of v2, /device:TPU:25, one launch (start us, length us, event | category | flops | bytes accessed | tf_op | source)
XLA Modules:
  0.0 91.2 jit_solution(1479200613221305900)
XLA Ops:
  0.6 1.3 %broadcast_in_dim.9.ngain_ref = bf16[1,2048]{1,0:T(2,128)(2,1)} reshape(bf16[2048]{0:T(1024)(128)(2,1)} %param.14) | data formatting | bytes 8192 | tf_op jit(solution)/shard_map/broadcast_in_dim | solution.py:555
  1.9 85.1 %shard_map.121 = (bf16[1,256,2048]{2,1,0:T(8,128)(2,1)}, bf16[1,256,512]{2,1,0:T(8,128)(2,1)}, bf16[1,256,512]{2,1,0:T(8,128)(2,1)}) custom-call(s32[4]{0:T(128)} %owner_ref.1, f32[1,128]{1,0:T(1,128)} %constant.2.clone.freq_ref, bf16[1,256,2048]{2,1,0:T(8,128)(2,1)} %hidden_ref.1, s32[1,256]{1,0:T(1,128)} %ids_ref.1, bf16[1,32,1024]{2,1,0:T(8,128)(2,1)} %prefix_ref.1, ...), custom_call_target="tpu_custom_call" | custom-call | tf_op jit(solution)/shard_map/pallas_call | solution.py:522
  87.1 0.0 copy-start.1
  87.1 2.3 %copy.16 = bf16[1,256,2048]{2,1,0:T(8,128)(2,1)} copy(bf16[1,256,2048]{2,1,0:T(8,128)(2,1)} %get-tuple-element.6) | data formatting | bytes 2097152
  89.4 0.0 copy-done.1
  89.4 0.0 copy-start
  89.4 0.7 copy.17
  90.1 0.3 copy-done
  90.5 0.7 copy.18
Async XLA Ops:
  87.1 2.4 %copy-start.1 = (bf16[1,256,512]{2,1,0:T(8,128)(2,1)S(1)}, bf16[1,256,512]{2,1,0:T(8,128)(2,1)}, u32[]{:S(2)}) copy-start(bf16[1,256,512]{2,1,0:T(8,128)(2,1)} %get-tuple-element.7) | copy-start | bytes 786436
  89.4 1.0 %copy-start = (bf16[1,256,512]{2,1,0:T(8,128)(2,1)S(1)}, bf16[1,256,512]{2,1,0:T(8,128)(2,1)}, u32[]{:S(2)}) copy-start(bf16[1,256,512]{2,1,0:T(8,128)(2,1)} %get-tuple-element.8) | copy-start | bytes 786436

commit v3 on v2

--- a/solution.py
+++ b/solution.py
@@ -28,27 +28,33 @@
         self.gy = (g + 2) % 4
         self.gd = (self.gx + 2) % 4
         width = buf.shape[2] if width is None else width
-        self.whole = (base, width)
-        if split:
+        rows = buf.shape[1]
+        self.whole = (0, rows, base, width)
+        if not split:
+            self.ranges = (self.whole,)
+            return
+        if rows % 128 == 0:
+            q = rows // 4
+            parts = [(i * q, q, base, width) for i in (self.g, self.gx, self.gy, self.gd)]
+        else:
             q = width // 4
-            self.ranges = (
-                (base + self.g * q, q),
-                (base + self.gx * q, q),
-                (base + self.gy * q, q),
-                (base + self.gd * q, q // 2),
-                (base + self.gd * q + q // 2, q // 2),
-            )
-        else:
-            self.ranges = (self.whole,)
-
-    def at(self, ref, lo, width):
-        if isinstance(lo, int):
-            return ref.at[:, pl.ds(lo, width)]
-        return ref.at[:, pl.ds(pl.multiple_of(lo, 128), width)]
-
-    def copy(self, zz, core, lo, width, s, r, dev, own=False):
-        place = self.at(self.buf.at[zz * 2 + core], lo, width)
-        src = self.at(self.own, lo, width) if own else place
+            parts = [(0, rows, base + i * q, q) for i in (self.g, self.gx, self.gy, self.gd)]
+        self.ranges = tuple(parts[:3]) + tuple(self.half(parts[3], i) for i in range(2))
+
+    def half(self, part, i):
+        row, rows, col, cols = part
+        if self.buf.shape[1] % 128 == 0:
+            return (row + i * (rows // 2), rows // 2, col, cols)
+        return (row, rows, col + i * (cols // 2), cols // 2)
+
+    def at(self, ref, row, rows, col, cols):
+        row = row if isinstance(row, int) else pl.multiple_of(row, 16)
+        col = col if isinstance(col, int) else pl.multiple_of(col, 128)
+        return ref.at[pl.ds(row, rows), pl.ds(col, cols)]
+
+    def copy(self, zz, core, part, s, r, dev, own=False):
+        place = self.at(self.buf.at[zz * 2 + core], *part)
+        src = self.at(self.own, *part) if own else place
         return pltpu.make_async_remote_copy(
             src_ref=src,
             dst_ref=place,
@@ -66,33 +72,31 @@
         return (self.g, self.z * 2 + 1 - self.c)
 
     def up(self, zz, own=False):
-        return self.copy(zz, self.c, *self.ranges[0], 0, 0, self.dev_z(self.z + 1), own)
+        return self.copy(zz, self.c, self.ranges[0], 0, 0, self.dev_z(self.z + 1), own)
 
     def down(self, zz, own=False):
-        return self.copy(zz, self.c, *self.ranges[0], 1 if own else 0, 0, self.dev_z(self.z - 1), own)
+        return self.copy(zz, self.c, self.ranges[0], 1 if own else 0, 0, self.dev_z(self.z - 1), own)
 
     def to_x(self, zz):
-        return self.copy(zz, self.c, *self.ranges[0], 1, 1, (self.gx, self.t))
+        return self.copy(zz, self.c, self.ranges[0], 1, 1, (self.gx, self.t))
 
     def to_y(self, zz):
-        return self.copy(zz, self.c, *self.ranges[0], 2, 2, (self.gy, self.t))
+        return self.copy(zz, self.c, self.ranges[0], 2, 2, (self.gy, self.t))
 
     def on_y(self, zz):
-        lo, width = self.ranges[1]
-        return self.copy(zz, self.c, lo, width // 2, 3, 3, (self.gy, self.t))
+        return self.copy(zz, self.c, self.half(self.ranges[1], 0), 3, 3, (self.gy, self.t))
 
     def on_x(self, zz):
-        lo, width = self.ranges[2]
-        return self.copy(zz, self.c, lo + width // 2, width // 2, 4, 4, (self.gx, self.t))
+        return self.copy(zz, self.c, self.half(self.ranges[2], 1), 4, 4, (self.gx, self.t))
 
     def across(self, zz, kind):
-        return self.copy(zz, self.c, *self.ranges[kind], 5 + kind, 5 + kind, self.sibling)
+        return self.copy(zz, self.c, self.ranges[kind], 5 + kind, 5 + kind, self.sibling)
 
     def across_own(self):
-        return self.copy(self.z, self.c, *self.whole, 5, 5, self.sibling, True)
+        return self.copy(self.z, self.c, self.whole, 5, 5, self.sibling, True)
 
     def wait_recv(self, zz, kind):
-        self.copy(zz, self.c, *self.ranges[kind], kind, kind, self.sibling).wait_recv()
+        self.copy(zz, self.c, self.ranges[kind], kind, kind, self.sibling).wait_recv()
 
     def start(self):
         @pl.when(self.z + 1 < self.nz)
@@ -153,14 +157,13 @@
             @pl.when(zz != self.z)
             def _():
                 for kind in range(len(self.ranges)):
-                    lo, width = self.ranges[kind]
                     self.copy(
-                        zz, 1 - self.c, lo, width, 5 + kind, 5 + kind, self.sibling
+                        zz, 1 - self.c, self.ranges[kind], 5 + kind, 5 + kind, self.sibling
                     ).wait_recv()
 
             @pl.when(zz == self.z)
             def _():
-                self.copy(zz, 1 - self.c, *self.whole, 5, 5, self.sibling).wait_recv()
+                self.copy(zz, 1 - self.c, self.whole, 5, 5, self.sibling).wait_recv()
 
             return carry
 
@@ -288,7 +291,7 @@
         at = pl.ds(pl.multiple_of(i * 64, 64), 64)
         x = hidden_ref[0, at, :].astype(jnp.float32)
         x = x * lax.rsqrt(jnp.mean(x * x, axis=-1, keepdims=True) + epsilon)
-        normed[at, :] = (x * ngain_ref[...].astype(jnp.float32)).astype(jnp.bfloat16)
+        normed[at, :] = (x * ngain_ref[...].astype(jnp.float32).reshape(1, -1)).astype(jnp.bfloat16)
         return carry
 
     lax.fori_loop(0, rows // 64, norm_rows, 0)
@@ -338,7 +341,6 @@
         return carry
 
     lax.fori_loop(1, nz, second, 0)
-    og.start()
     kg.finish()
 
     def project(j):
@@ -396,11 +398,11 @@
     def _():
         beside.start()
 
+    og.start()
+
     def third(s, carry):
         pg.both(s, pg.arrive)
-        og.both(s, og.arrive)
         qg.step(s + 1)
-        og.both(s, og.spread)
         return carry
 
     lax.fori_loop(1, nz, third, 0)
@@ -408,6 +410,14 @@
     qg.finish()
     lax.fori_loop(0, qw // BLOCK, query_block, 0)
     pg.finish()
+
+    def fourth(s, carry):
+        og.both(s, og.arrive)
+        og.both(s, og.spread)
+        og.step(s)
+        return carry
+
+    fourth(1, 0)
 
     @pl.when(t >= 2)
     def _():
@@ -459,10 +469,6 @@
                 r * rows:(r + 1) * rows
             ]
 
-        def fourth(s, carry):
-            og.step(s)
-            return carry
-
         lax.fori_loop(2 + h * per, jnp.minimum(2 + (h + 1) * per, nz + 2), fourth, 0)
         return carry
 
@@ -500,6 +506,18 @@
     @pl.when((c == 1) & (z > 0))
     def _():
         passed_on.wait_send()
+
+
+def place(*refs):
+    count = (len(refs) - 1) // 2
+    sems = refs[-1]
+    copies = [
+        pltpu.make_async_copy(refs[i], refs[count + i], sems.at[i]) for i in range(count)
+    ]
+    for one in copies:
+        one.start()
+    for one in copies:
+        one.wait()
 
 
 def per_device(
@@ -519,7 +537,7 @@
     bf = jnp.bfloat16
     vm = pl.BlockSpec(memory_space=pltpu.VMEM)
     dma = pltpu.SemaphoreType.DMA
-    return pl.pallas_call(
+    made = pl.pallas_call(
         functools.partial(kernel, nt, ng),
         out_shape=(
             jax.ShapeDtypeStruct((1, rows, w_out.shape[1]), bf),
@@ -552,8 +570,17 @@
         ),
     )(
         prefix_owner, jnp.asarray(freqs), hidden_in, doc_ids, prefix_kv,
-        norm_gain[None], query_gain[None], key_norm_gain[None], w_qkv, w_out,
+        norm_gain, query_gain[None], key_norm_gain[None], w_qkv, w_out,
     )
+    anywhere = pl.BlockSpec(memory_space=pl.ANY)
+    return pl.pallas_call(
+        place,
+        out_shape=tuple(jax.ShapeDtypeStruct(x.shape, x.dtype) for x in made),
+        in_specs=[anywhere] * len(made),
+        out_specs=(anywhere,) * len(made),
+        scratch_shapes=[dma((len(made),))],
+        compiler_params=pltpu.CompilerParams(vmem_limit_bytes=63 * 1024 * 1024),
+    )(*made)
 
 
 def solution(mesh):

time: 91.4 us -> 133 us (1.46)
  Pallas kernels: 85.1 us -> 131 us
  local copies, waits for them, and re-layouts: 5.39 us -> 0 us
    pallas_call x0 -> x1, Pallas kernels: none -> 48.8 us  [per_device(): pl.pallas_call(place, out_shape=tuple((jax.ShapeDtypeStruct(x.shape, x.dt...]
    unnamed x7 -> x0, local copies, waits for them, and re-layouts: 4.1 us -> none
    pallas_call x1, Pallas kernels: 85.1 us -> 82.5 us  [per_device(): pl.pallas_call(functools.partial(kernel, nt, ng), out_shape=(jax.ShapeDty...]
where the time goes in v3:
time: 133 us; the launch traced here: 132 us
  Pallas kernels  131 us (98%)
    pallas_call x1, Pallas kernels, per_device(): pl.pallas_call(functools.partial(kernel, nt, ng), out_shape=(jax.ShapeDty...  82.5 us
    pallas_call x1, Pallas kernels, per_device(): pl.pallas_call(place, out_shape=tuple((jax.ShapeDtypeStruct(x.shape, x.dt...  48.8 us

profile of v3, /device:TPU:25, one launch (start us, length us, event | category | flops | bytes accessed | tf_op | source)
XLA Modules:
  0.0 132.0 jit_solution(2148136264387778901)
XLA Ops:
  0.6 82.5 %shard_map.121 = (bf16[1,256,2048]{2,1,0:T(8,128)(2,1)}, bf16[1,256,512]{2,1,0:T(8,128)(2,1)}, bf16[1,256,512]{2,1,0:T(8,128)(2,1)}) custom-call(s32[4]{0:T(128)} %owner_ref.1, f32[1,128]{1,0:T(1,128)} %constant.2.clone.freq_ref, bf16[1,256,2048]{2,1,0:T(8,128)(2,1)} %hidden_ref.1, s32[1,256]{1,0:T(1,128)} %ids_ref.1, bf16[1,32,1024]{2,1,0:T(8,128)(2,1)} %prefix_ref.1, ...), custom_call_target="tpu_custom_call" | custom-call | tf_op jit(solution)/shard_map/pallas_call | solution.py:540
  83.2 48.8 %shard_map.122 = (bf16[1,256,2048]{2,1,0:T(8,128)(2,1)}, bf16[1,256,512]{2,1,0:T(8,128)(2,1)}, bf16[1,256,512]{2,1,0:T(8,128)(2,1)}) custom-call(bf16[1,256,2048]{2,1,0:T(8,128)(2,1)} %get-tuple-element.6.refs_0_, bf16[1,256,512]{2,1,0:T(8,128)(2,1)} %get-tuple-element.7.refs_1_, bf16[1,256,512]{2,1,0:T(8,128)(2,1)} %get-tuple-element.8.refs_2_), custom_call_target="tpu_custom_call" | custom-call | tf_op jit(solution)/shard_map/pallas_call | solution.py:576

commit v4 on v3

--- a/solution.py
+++ b/solution.py
@@ -33,18 +33,12 @@
         if not split:
             self.ranges = (self.whole,)
             return
-        if rows % 128 == 0:
-            q = rows // 4
-            parts = [(i * q, q, base, width) for i in (self.g, self.gx, self.gy, self.gd)]
-        else:
-            q = width // 4
-            parts = [(0, rows, base + i * q, q) for i in (self.g, self.gx, self.gy, self.gd)]
+        q = width // 4
+        parts = [(0, rows, base + i * q, q) for i in (self.g, self.gx, self.gy, self.gd)]
         self.ranges = tuple(parts[:3]) + tuple(self.half(parts[3], i) for i in range(2))
 
     def half(self, part, i):
         row, rows, col, cols = part
-        if self.buf.shape[1] % 128 == 0:
-            return (row + i * (rows // 2), rows // 2, col, cols)
         return (row, rows, col + i * (cols // 2), cols // 2)
 
     def at(self, ref, row, rows, col, cols):
@@ -341,6 +335,7 @@
         return carry
 
     lax.fori_loop(1, nz, second, 0)
+    og.start()
     kg.finish()
 
     def project(j):
@@ -376,7 +371,12 @@
         queries[:, at] = turned(project(j), qgain_ref[...].astype(jnp.float32))
         return carry
 
+    def out_arrive(s, carry):
+        og.both(s, og.arrive)
+        return carry
+
     lax.fori_loop(0, kvw // BLOCK, key_block, 0)
+    out_arrive(1, 0)
     lax.fori_loop(0, kvw // BLOCK, value_block, 0)
 
     def kv_copy(src, dst, dev):
@@ -398,26 +398,28 @@
     def _():
         beside.start()
 
-    og.start()
-
     def third(s, carry):
         pg.both(s, pg.arrive)
         qg.step(s + 1)
         return carry
 
     lax.fori_loop(1, nz, third, 0)
+    lax.fori_loop(2, nz, out_arrive, 0)
+
+    def out_spread(s, carry):
+        og.both(s, og.spread)
+        return carry
+
+    lax.fori_loop(1, nz, out_spread, 0)
     qg.step(nz + 1)
     qg.finish()
     lax.fori_loop(0, qw // BLOCK, query_block, 0)
     pg.finish()
 
     def fourth(s, carry):
-        og.both(s, og.arrive)
-        og.both(s, og.spread)
         og.step(s)
         return carry
 
-    fourth(1, 0)
 
     @pl.when(t >= 2)
     def _():
@@ -509,15 +511,9 @@
 
 
 def place(*refs):
-    count = (len(refs) - 1) // 2
-    sems = refs[-1]
-    copies = [
-        pltpu.make_async_copy(refs[i], refs[count + i], sems.at[i]) for i in range(count)
-    ]
-    for one in copies:
-        one.start()
-    for one in copies:
-        one.wait()
+    count = len(refs) // 2
+    for src, dst in zip(refs[:count], refs[count:]):
+        dst[...] = src[...]
 
 
 def per_device(
@@ -572,13 +568,15 @@
         prefix_owner, jnp.asarray(freqs), hidden_in, doc_ids, prefix_kv,
         norm_gain, query_gain[None], key_norm_gain[None], w_qkv, w_out,
     )
-    anywhere = pl.BlockSpec(memory_space=pl.ANY)
+    parts = [
+        pl.BlockSpec((1, rows // 4, x.shape[2]), lambda i: (0, i, 0)) for x in made
+    ]
     return pl.pallas_call(
         place,
+        grid=(4,),
         out_shape=tuple(jax.ShapeDtypeStruct(x.shape, x.dtype) for x in made),
-        in_specs=[anywhere] * len(made),
-        out_specs=(anywhere,) * len(made),
-        scratch_shapes=[dma((len(made),))],
+        in_specs=parts,
+        out_specs=tuple(parts),
         compiler_params=pltpu.CompilerParams(vmem_limit_bytes=63 * 1024 * 1024),
     )(*made)
 

time: 133 us -> 88.3 us (0.66)
  Pallas kernels: 131 us -> 87.4 us
    pallas_call x1, Pallas kernels: 48.8 us -> 3.55 us  [per_device(): pl.pallas_call(place, grid=(4,), out_shape=tuple((jax.ShapeDtypeStruct(x....]
where the time goes in v4:
time: 88.3 us; the launch traced here: 88.1 us
  Pallas kernels  87.4 us (99%)
    pallas_call x1, Pallas kernels, per_device(): pl.pallas_call(functools.partial(kernel, nt, ng), out_shape=(jax.ShapeDty...  83.9 us
    pallas_call x1, Pallas kernels, per_device(): pl.pallas_call(place, grid=(4,), out_shape=tuple((jax.ShapeDtypeStruct(x....  3.55 us

profile of v4, /device:TPU:25, one launch (start us, length us, event | category | flops | bytes accessed | tf_op | source)
XLA Modules:
  0.0 88.1 jit_solution(7481778709782830528)
XLA Ops:
  0.6 83.9 %shard_map.121 = (bf16[1,256,2048]{2,1,0:T(8,128)(2,1)}, bf16[1,256,512]{2,1,0:T(8,128)(2,1)}, bf16[1,256,512]{2,1,0:T(8,128)(2,1)}) custom-call(s32[4]{0:T(128)} %owner_ref.1, f32[1,128]{1,0:T(1,128)} %constant.2.clone.freq_ref, bf16[1,256,2048]{2,1,0:T(8,128)(2,1)} %hidden_ref.1, s32[1,256]{1,0:T(1,128)} %ids_ref.1, bf16[1,32,1024]{2,1,0:T(8,128)(2,1)} %prefix_ref.1, ...), custom_call_target="tpu_custom_call" | custom-call | tf_op jit(solution)/shard_map/pallas_call | solution.py:536
  84.5 3.6 %shard_map.122 = (bf16[1,256,2048]{2,1,0:T(8,128)(2,1)}, bf16[1,256,512]{2,1,0:T(8,128)(2,1)}, bf16[1,256,512]{2,1,0:T(8,128)(2,1)}) custom-call(bf16[1,256,2048]{2,1,0:T(8,128)(2,1)} %get-tuple-element.6.refs_0_, bf16[1,256,512]{2,1,0:T(8,128)(2,1)} %get-tuple-element.7.refs_1_, bf16[1,256,512]{2,1,0:T(8,128)(2,1)} %get-tuple-element.8.refs_2_), custom_call_target="tpu_custom_call" | custom-call | tf_op jit(solution)/shard_map/pallas_call | solution.py:574

commit v5 on v4

--- a/solution.py
+++ b/solution.py
@@ -421,6 +421,15 @@
         return carry
 
 
+    for one in (kg, qg, pg):
+        one.sent()
+    for k in range(1, ng):
+        prefix_copy(k).wait_send()
+    for back in range(1, REACH + 1):
+        @pl.when(t + back < nt)
+        def _():
+            id_copy(back).wait_send()
+
     @pl.when(t >= 2)
     def _():
         to_next.wait_recv()
@@ -488,14 +497,7 @@
 
     lax.fori_loop(0, out_ref.shape[2] // BLOCK, out_block, 0)
 
-    for one in (kg, qg, og, pg):
-        one.sent()
-    for k in range(1, ng):
-        prefix_copy(k).wait_send()
-    for back in range(1, REACH + 1):
-        @pl.when(t + back < nt)
-        def _():
-            id_copy(back).wait_send()
+    og.sent()
 
     @pl.when(t + 2 < nt)
     def _():
@@ -511,9 +513,15 @@
 
 
 def place(*refs):
-    count = len(refs) // 2
-    for src, dst in zip(refs[:count], refs[count:]):
-        dst[...] = src[...]
+    count = (len(refs) - 1) // 2
+    sems = refs[-1]
+    copies = [
+        pltpu.make_async_copy(refs[i], refs[count + i], sems.at[i]) for i in range(count)
+    ]
+    for one in copies:
+        one.start()
+    for one in copies:
+        one.wait()
 
 
 def per_device(
@@ -536,9 +544,9 @@
     made = pl.pallas_call(
         functools.partial(kernel, nt, ng),
         out_shape=(
-            jax.ShapeDtypeStruct((1, rows, w_out.shape[1]), bf),
-            jax.ShapeDtypeStruct((1, rows, kvw), bf),
-            jax.ShapeDtypeStruct((1, rows, kvw), bf),
+            pltpu.VMEM((1, rows, w_out.shape[1]), bf),
+            pltpu.VMEM((1, rows, kvw), bf),
+            pltpu.VMEM((1, rows, kvw), bf),
         ),
         in_specs=[pl.BlockSpec(memory_space=pltpu.SMEM)] + [vm] * 9,
         out_specs=(vm, vm, vm),
@@ -568,16 +576,12 @@
         prefix_owner, jnp.asarray(freqs), hidden_in, doc_ids, prefix_kv,
         norm_gain, query_gain[None], key_norm_gain[None], w_qkv, w_out,
     )
-    parts = [
-        pl.BlockSpec((1, rows // 4, x.shape[2]), lambda i: (0, i, 0)) for x in made
-    ]
     return pl.pallas_call(
         place,
-        grid=(4,),
         out_shape=tuple(jax.ShapeDtypeStruct(x.shape, x.dtype) for x in made),
-        in_specs=parts,
-        out_specs=tuple(parts),
-        compiler_params=pltpu.CompilerParams(vmem_limit_bytes=63 * 1024 * 1024),
+        in_specs=[vm] * len(made),
+        out_specs=(pl.BlockSpec(memory_space=pl.ANY),) * len(made),
+        scratch_shapes=[dma((len(made),))],
     )(*made)
 
 

time: 88.3 us -> 88.4 us (level)
  local copies, waits for them, and re-layouts: 0 us -> 2.38 us
  Pallas kernels: 87.4 us -> 85.2 us
    unnamed x0 -> x6, local copies, waits for them, and re-layouts: none -> 2.38 us
    pallas_call x2, Pallas kernels: 87.4 us -> 85.2 us  [the longest x1 82.7 us: per_device(): pl.pallas_call(functools.partial(kernel, nt, ng), out_shape=(pltpu.VMEM((...]
where the time goes in v5:
time: 88.4 us; the launch traced here: 88.2 us
  Pallas kernels  85.2 us (96%)
  local copies, waits for them, and re-layouts  2.38 us (3%)
    pallas_call x1, Pallas kernels, per_device(): pl.pallas_call(functools.partial(kernel, nt, ng), out_shape=(pltpu.VMEM((...  82.7 us
    pallas_call x1, Pallas kernels, per_device(): pl.pallas_call(place, out_shape=tuple((jax.ShapeDtypeStruct(x.shape, x.dt...  2.5 us
    unnamed x6, local copies, waits for them, and re-layouts  2.38 us

profile of v5, /device:TPU:25, one launch (start us, length us, event | category | flops | bytes accessed | tf_op | source)
XLA Modules:
  0.0 88.2 jit_solution(14858197471545196512)
XLA Ops:
  0.6 82.7 %shard_map.121 = (bf16[1,256,2048]{2,1,0:T(8,128)(2,1)S(1)}, bf16[1,256,512]{2,1,0:T(8,128)(2,1)S(1)}, bf16[1,256,512]{2,1,0:T(8,128)(2,1)S(1)}) custom-call(s32[4]{0:T(128)} %owner_ref.1, f32[1,128]{1,0:T(1,128)} %constant.2.clone.freq_ref, bf16[1,256,2048]{2,1,0:T(8,128)(2,1)} %hidden_ref.1, s32[1,256]{1,0:T(1,128)} %ids_ref.1, ...), custom_call_target="tpu_custom_call" | custom-call | tf_op jit(solution)/shard_map/pallas_call | solution.py:544
  83.3 0.0 copy-start
  83.3 1.0 %copy-done = bf16[1,256,2048]{2,1,0:T(8,128)(2,1)} copy-done((bf16[1,256,2048]{2,1,0:T(8,128)(2,1)}, bf16[1,256,2048]{2,1,0:T(8,128)(2,1)S(1)}, u32[]{:S(2)}) %copy-start) | copy-done | bytes 1048600
  84.3 0.0 copy-start.1
  84.3 0.7 copy-done.1
  85.0 0.0 copy-start.2
  85.0 0.7 copy-done.2
  85.7 2.5 %shard_map.122 = (bf16[1,256,2048]{2,1,0:T(8,128)(2,1)}, bf16[1,256,512]{2,1,0:T(8,128)(2,1)}, bf16[1,256,512]{2,1,0:T(8,128)(2,1)}) custom-call(bf16[1,256,2048]{2,1,0:T(8,128)(2,1)} %copy-done, bf16[1,256,512]{2,1,0:T(8,128)(2,1)} %copy-done.1, bf16[1,256,512]{2,1,0:T(8,128)(2,1)} %copy-done.2), custom_call_target="tpu_custom_call" | custom-call | tf_op jit(solution)/shard_map/pallas_call | solution.py:579
Async XLA Ops:
  83.3 1.0 %copy-start = (bf16[1,256,2048]{2,1,0:T(8,128)(2,1)}, bf16[1,256,2048]{2,1,0:T(8,128)(2,1)S(1)}, u32[]{:S(2)}) copy-start(bf16[1,256,2048]{2,1,0:T(8,128)(2,1)S(1)} %get-tuple-element.6.refs_0_) | copy-start | bytes 3145732
  84.3 0.7 copy-start.1
  85.0 0.7 copy-start.2

commit v6 on v5

--- a/solution.py
+++ b/solution.py
@@ -515,9 +515,16 @@
 def place(*refs):
     count = (len(refs) - 1) // 2
     sems = refs[-1]
-    copies = [
-        pltpu.make_async_copy(refs[i], refs[count + i], sems.at[i]) for i in range(count)
-    ]
+    copies = []
+    for i in range(count):
+        rows = refs[i].shape[1] // 4
+        for j in range(4):
+            at = pl.ds(j * rows, rows)
+            copies.append(
+                pltpu.make_async_copy(
+                    refs[i].at[:, at], refs[count + i].at[:, at], sems.at[i, j]
+                )
+            )
     for one in copies:
         one.start()
     for one in copies:
@@ -581,7 +588,8 @@
         out_shape=tuple(jax.ShapeDtypeStruct(x.shape, x.dtype) for x in made),
         in_specs=[vm] * len(made),
         out_specs=(pl.BlockSpec(memory_space=pl.ANY),) * len(made),
-        scratch_shapes=[dma((len(made),))],
+        scratch_shapes=[dma((len(made), 4))],
+        compiler_params=pltpu.CompilerParams(vmem_limit_bytes=1024 * 1024),
     )(*made)
 
 

time: 88.4 us -> 84.7 us (0.958)
  local copies, waits for them, and re-layouts: 2.38 us -> 0 us
  Pallas kernels: 85.2 us -> 83.9 us
    unnamed x6 -> x0, local copies, waits for them, and re-layouts: 2.38 us -> none
    pallas_call x1, Pallas kernels: 2.5 us -> 1.23 us  [per_device(): pl.pallas_call(place, out_shape=tuple((jax.ShapeDtypeStruct(x.shape, x.dt...]
where the time goes in v6:
time: 84.7 us; the launch traced here: 84.6 us
  Pallas kernels  83.9 us (99%)
    pallas_call x1, Pallas kernels, per_device(): pl.pallas_call(functools.partial(kernel, nt, ng), out_shape=(pltpu.VMEM((...  82.7 us

profile of v6, /device:TPU:25, one launch (start us, length us, event | category | flops | bytes accessed | tf_op | source)
XLA Modules:
  0.0 84.6 jit_solution(17407640772384309290)
XLA Ops:
  0.6 82.7 %shard_map.121 = (bf16[1,256,2048]{2,1,0:T(8,128)(2,1)S(1)}, bf16[1,256,512]{2,1,0:T(8,128)(2,1)S(1)}, bf16[1,256,512]{2,1,0:T(8,128)(2,1)S(1)}) custom-call(s32[4]{0:T(128)} %owner_ref.1, f32[1,128]{1,0:T(1,128)} %constant.2.clone.freq_ref, bf16[1,256,2048]{2,1,0:T(8,128)(2,1)} %hidden_ref.1, s32[1,256]{1,0:T(1,128)} %ids_ref.1, ...), custom_call_target="tpu_custom_call" | custom-call | tf_op jit(solution)/shard_map/pallas_call | solution.py:551
  83.3 1.2 %shard_map.122 = (bf16[1,256,2048]{2,1,0:T(8,128)(2,1)}, bf16[1,256,512]{2,1,0:T(8,128)(2,1)}, bf16[1,256,512]{2,1,0:T(8,128)(2,1)}) custom-call(bf16[1,256,2048]{2,1,0:T(8,128)(2,1)S(1)} %get-tuple-element.6.refs_0_, bf16[1,256,512]{2,1,0:T(8,128)(2,1)S(1)} %get-tuple-element.7.refs_1_, bf16[1,256,512]{2,1,0:T(8,128)(2,1)S(1)} %get-tuple-element.8.refs_2_), custom_call_target="tpu_custom_call" | custom-call | tf_op jit(solution)/shard_map/pallas_call | solution.py:586

commit v7 on v6

--- a/solution.py
+++ b/solution.py
@@ -401,16 +401,15 @@
     def third(s, carry):
         pg.both(s, pg.arrive)
         qg.step(s + 1)
+
+        @pl.when(s >= 2)
+        def _():
+            og.both(s, og.arrive)
+
+        og.both(s, og.spread)
         return carry
 
     lax.fori_loop(1, nz, third, 0)
-    lax.fori_loop(2, nz, out_arrive, 0)
-
-    def out_spread(s, carry):
-        og.both(s, og.spread)
-        return carry
-
-    lax.fori_loop(1, nz, out_spread, 0)
     qg.step(nz + 1)
     qg.finish()
     lax.fori_loop(0, qw // BLOCK, query_block, 0)

time: 84.7 us -> 84.5 us (level)
  no operation moved by 1% of the time
where the time goes in v7:
time: 84.5 us; the launch traced here: 84.3 us
  Pallas kernels  83.7 us (99%)
    pallas_call x1, Pallas kernels, per_device(): pl.pallas_call(functools.partial(kernel, nt, ng), out_shape=(pltpu.VMEM((...  82.5 us

profile of v7, /device:TPU:25, one launch (start us, length us, event | category | flops | bytes accessed | tf_op | source)
XLA Modules:
  0.0 84.3 jit_solution(14372811473034109135)
XLA Ops:
  0.6 82.5 %shard_map.121 = (bf16[1,256,2048]{2,1,0:T(8,128)(2,1)S(1)}, bf16[1,256,512]{2,1,0:T(8,128)(2,1)S(1)}, bf16[1,256,512]{2,1,0:T(8,128)(2,1)S(1)}) custom-call(s32[4]{0:T(128)} %owner_ref.1, f32[1,128]{1,0:T(1,128)} %constant.2.clone.freq_ref, bf16[1,256,2048]{2,1,0:T(8,128)(2,1)} %hidden_ref.1, s32[1,256]{1,0:T(1,128)} %ids_ref.1, ...), custom_call_target="tpu_custom_call" | custom-call | tf_op jit(solution)/shard_map/pallas_call | solution.py:550
  83.1 1.2 %shard_map.122 = (bf16[1,256,2048]{2,1,0:T(8,128)(2,1)}, bf16[1,256,512]{2,1,0:T(8,128)(2,1)}, bf16[1,256,512]{2,1,0:T(8,128)(2,1)}) custom-call(bf16[1,256,2048]{2,1,0:T(8,128)(2,1)S(1)} %get-tuple-element.6.refs_0_, bf16[1,256,512]{2,1,0:T(8,128)(2,1)S(1)} %get-tuple-element.7.refs_1_, bf16[1,256,512]{2,1,0:T(8,128)(2,1)S(1)} %get-tuple-element.8.refs_2_), custom_call_target="tpu_custom_call" | custom-call | tf_op jit(solution)/shard_map/pallas_call | solution.py:585
